TPU v7x, 512 devices: a whole 4x4x16 slice. The times are simulated.
512 devices in a mesh: row: 64 (over y, z), col: 8 (over x, core).
Axes of the slice: x: 4, y: 4, z: 16, core: 2. Of those that a mesh axis runs over, the one named last changes fastest.
Arguments:
- earlier_vectors: bfloat16 [16384, 1536], P(('row', 'col')), may hold values from -0.4082483 to 0.4082483
- later_vectors: bfloat16 [8192, 1536], P(('row', 'col')), may hold values from -0.4082483 to 0.4082483
Outputs:
- mixed_dual_left: float32 [16384], P(('row', 'col'))
- mixed_dual_right: float32 [8192], P(('row', 'col'))
- earlier_symmetric_dual: float32 [16384], P(('row', 'col'))
- later_symmetric_dual: float32 [8192], P(('row', 'col'))
- divergence: float32 [], replicated
All inputs are finite; a program needn't handle non-finite values.
Results may differ from a plain program's by a relative error of at most 0.0003.
Values may be sent and summed in bfloat16 or wider, within the bound.
A program may use at most 64 MiB of HBM per device.

v0:
```python
import jax
import jax.numpy as jnp
from jax import lax
from jax.sharding import PartitionSpec as P

ITERS = 2


EPSILON = 0.04


def combined_all(x, axis, combine):
    everything = jax.tree.map(lambda part: lax.all_gather(part, axis), x)
    initial = jax.tree.map(lambda part: part[0], everything)

    def step(k, so_far):
        return combine(so_far, jax.tree.map(lambda part: part[k], everything))

    return lax.fori_loop(1, lax.axis_size(axis), step, initial)


def squares(values):
    return jnp.einsum("ij,ij->i", values, values, preferred_element_type=jnp.float32)


def cost_tile(source_weights, target_weights):
    cross = jnp.dot(source_weights, target_weights.T, preferred_element_type=jnp.float32)
    return 0.5 * squares(source_weights)[:, None] + 0.5 * squares(target_weights)[None, :] - cross


def join_stats(first, second):
    joined = []
    for index in range(0, len(first), 2):
        top = jnp.maximum(first[index], second[index])
        total = first[index + 1] * jnp.exp(first[index] - top) + second[index + 1] * jnp.exp(
            second[index] - top
        )
        joined.append(top)
        joined.append(total)
    return tuple(joined)


def per_device(earlier_vectors, later_vectors):
    row_src, row_tgt = (
        lax.all_gather(earlier_vectors, "col", axis=0, tiled=True),
        lax.all_gather(later_vectors, "col", axis=0, tiled=True),
    )
    col_src, col_tgt = (
        lax.all_gather(earlier_vectors, "row", axis=0, tiled=True),
        lax.all_gather(later_vectors, "row", axis=0, tiled=True),
    )
    rows_ax = lax.axis_size("row")
    cols_ax = lax.axis_size("col")
    row_pos = lax.axis_index("row")
    col_pos = lax.axis_index("col")
    count_src = earlier_vectors.shape[0] * rows_ax * cols_ax
    count_tgt = later_vectors.shape[0] * rows_ax * cols_ax
    log_src = -jnp.log(jnp.float32(count_src))
    log_tgt = -jnp.log(jnp.float32(count_tgt))
    costs = (cost_tile(row_src, col_tgt), cost_tile(row_src, col_src), cost_tile(row_tgt, col_tgt))
    row_logs = (log_tgt, log_src, log_tgt)
    col_logs = (log_src, log_src, log_tgt)
    col_pots = tuple((jnp.zeros((tile.shape[1],), jnp.float32) for tile in costs))
    row_pots = tuple((jnp.zeros((tile.shape[0],), jnp.float32) for tile in costs))
    for step_index in range(ITERS):
        tops = []
        totals = []
        for tile, pot in zip(costs, col_pots):
            score = (pot[None, :] - tile) / EPSILON
            top = jnp.max(score, axis=1)
            tops.append(top)
            totals.append(jnp.sum(jnp.exp(score - top[:, None]), axis=1))
        row_tops = lax.pmax((tops[0], tops[1], tops[2]), "col")
        scaled = tuple((totals[k] * jnp.exp(tops[k] - row_tops[k]) for k in range(3)))
        row_totals = lax.psum((scaled[0], scaled[1], scaled[2]), "col")
        row_pots = tuple(
            (-EPSILON * (row_logs[k] + row_tops[k] + jnp.log(row_totals[k])) for k in range(3))
        )
        tops = []
        totals = []
        for tile, pot in zip(costs, row_pots):
            back = (pot[:, None] - tile) / EPSILON
            top = jnp.max(back, axis=0)
            tops.append(top)
            totals.append(jnp.sum(jnp.exp(back - top[None, :]), axis=0))
        flat = combined_all(
            (tops[0], totals[0], tops[1], totals[1], tops[2], totals[2]), "row", join_stats
        )
        col_pots = tuple(
            (-EPSILON * (col_logs[k] + flat[2 * k] + jnp.log(flat[2 * k + 1])) for k in range(3))
        )
    own_rows = []
    for pot in row_pots:
        width = pot.shape[0] // cols_ax
        own_rows.append(lax.dynamic_slice_in_dim(pot, col_pos * width, width))
    own_cols = []
    for pot in col_pots:
        width = pot.shape[0] // rows_ax
        own_cols.append(lax.dynamic_slice_in_dim(pot, row_pos * width, width))
    sizes_rows = (count_src, count_src, count_tgt)
    sizes_cols = (count_tgt, count_src, count_tgt)
    partial_values = tuple(
        (
            jnp.sum(own_rows[k]) / sizes_rows[k] + jnp.sum(own_cols[k]) / sizes_cols[k]
            for k in range(3)
        )
    )
    totals_all = lax.psum((partial_values[0], partial_values[1], partial_values[2]), ("row", "col"))
    divergence = totals_all[0] - 0.5 * totals_all[1] - 0.5 * totals_all[2]
    return (own_rows[0], own_cols[0], own_rows[1], own_rows[2], divergence)


def solution(mesh):
    return jax.shard_map(
        per_device,
        mesh=mesh,
        in_specs=(P(("row", "col"), None), P(("row", "col"), None)),
        out_specs=(P(("row", "col")), P(("row", "col")), P(("row", "col")), P(("row", "col")), P()),
        check_vma=False,
    )
```

profile of v0, /device:TPU:1, one launch (start us, length us, event | category | flops | bytes accessed | tf_op | source)
XLA Modules:
  0.0 1856.9 jit_solution(17790834355647059218)
XLA Ops:
  8.7 19.9 %all_gather.95 = bf16[128,1536]{1,0:T(8,128)(2,1)S(1)} all-gather(bf16[16,1536]{1,0:T(8,128)(2,1)} %param.7), channel_id=1, replica_groups=mesh['row'=64,'col'=8] {'col'}, dimensions={0}, use_global_device_ids=true | all-gather | bytes 442368 | tf_op jit(solution)/shard_map/all_gather | solution.py:46
  28.7 13.7 all_gather.84
  42.7 108.8 %all-gather.15.cloned.1.call-done = bf16[1024,1536]{1,0:T(8,128)(2,1)} async-done(((bf16[16,1536]{1,0:T(8,128)(2,1)}), bf16[1024,1536]{1,0:T(8,128)(2,1)}) %all-gather.15.cloned.1.call-update) | async-done | bytes 3145744 | tf_op jit(solution)/shard_map/all_gather | solution.py:50
  151.5 2.7 fusion.1
  154.3 1.2 fusion.12
  156.6 1.1 fusion.7
  158.0 143.9 %all-gather.17.cloned.1.call-done = bf16[2048,1536]{1,0:T(8,128)(2,1)} async-done(((bf16[32,1536]{1,0:T(8,128)(2,1)}), bf16[2048,1536]{1,0:T(8,128)(2,1)}) %all-gather.17.cloned.1.call-update) | async-done | bytes 6291472 | tf_op jit(solution)/shard_map/all_gather | solution.py:49
  302.0 4.2 fusion
  306.6 3.1 fusion.2
  309.7 19.9 %all-reduce.4 = (f32[256]{0:T(256)S(1)}, f32[256]{0:T(256)S(1)}, f32[128]{0:T(128)S(1)}) all-reduce(f32[256]{0:T(256)S(1)} %get-tuple-element.738, f32[256]{0:T(256)S(1)} %get-tuple-element.740, f32[128]{0:T(128)S(1)} %get-tuple-element.742), channel_id=1, replica_groups=mesh['row'=64,'col'=8] {'col'}, use_global_device_ids=true, to_apply=%region_1.0 | all-reduce | flops 640 | bytes 5120 | tf_op jit(solution)/shard_map/pmax | solution.py:73
  330.2 12.4 all-reduce.2
  342.6 1.2 fusion.13
  343.8 1.2 exponential_reduce_fusion.10
  345.0 62.3 %all-gather.4 = f32[65536]{0:T(1024)S(1)} all-gather(f32[1024]{0:T(1024)S(1)} %fusion.13), channel_id=6, replica_groups=mesh['row'=64,'col'=8] {'row'}, dimensions={0}, use_global_device_ids=true | all-gather | bytes 266240 | tf_op jit(solution)/shard_map/all_gather | solution.py:13
  408.1 61.1 %all-gather.5 = f32[65536]{0:T(1024)S(1)} all-gather(f32[1024]{0:T(1024)S(1)} %exponential_reduce_fusion.10), channel_id=7, replica_groups=mesh['row'=64,'col'=8] {'row'}, dimensions={0}, use_global_device_ids=true | all-gather | bytes 266240 | tf_op jit(solution)/shard_map/all_gather | solution.py:13
  470.0 1.7 reshape.44
  472.2 64.6 %all-gather = f32[65536]{0:T(1024)S(1)} all-gather(f32[1024]{0:T(1024)S(1)} %fusion.8), channel_id=2, replica_groups=mesh['row'=64,'col'=8] {'row'}, dimensions={0}, use_global_device_ids=true | all-gather | bytes 266240 | tf_op jit(solution)/shard_map/all_gather | solution.py:13
  537.5 1.7 reshape.39
  539.2 61.8 %all-gather.1 = f32[65536]{0:T(1024)S(1)} all-gather(f32[1024]{0:T(1024)S(1)} %exponential_reduce_fusion.6), channel_id=3, replica_groups=mesh['row'=64,'col'=8] {'row'}, dimensions={0}, use_global_device_ids=true | all-gather | bytes 266240 | tf_op jit(solution)/shard_map/all_gather | solution.py:13
  601.8 1.0 reshape.40
  603.6 73.4 %all-gather.2 = f32[131072]{0:T(1024)S(1)} all-gather(f32[2048]{0:T(1024)S(1)} %fusion.3), channel_id=4, replica_groups=mesh['row'=64,'col'=8] {'row'}, dimensions={0}, use_global_device_ids=true | all-gather | bytes 532480 | tf_op jit(solution)/shard_map/all_gather | solution.py:13
  677.8 2.0 reshape.41
  679.8 70.7 %all-gather.3 = f32[131072]{0:T(1024)S(1)} all-gather(f32[2048]{0:T(1024)S(1)} %exponential_reduce_fusion.2), channel_id=5, replica_groups=mesh['row'=64,'col'=8] {'row'}, dimensions={0}, use_global_device_ids=true | all-gather | bytes 532480 | tf_op jit(solution)/shard_map/all_gather | solution.py:13
  751.4 1.9 reshape.42
  753.3 205.7 %while.50 = (s32[]{:T(128)}, f32[1024]{0:T(1024)S(1)}, f32[1024]{0:T(1024)S(1)}, f32[2048]{0:T(1024)S(1)}, f32[2048]{0:T(1024)S(1)}, /*index=5*/f32[1024]{0:T(10...) while((s32[]{:T(128)}, f32[1024]{0:T(1024)S(1)}, ...), condition=%wide.region_19.0_spmd, body=%wide.region_18.0_spmd.sunk | while | flops 24581 | bytes 164043 | solution.py:19
  755.7 0.9 constant_dynamic-slice_fusion.26
  758.9 0.9 constant_dynamic-slice_fusion.26
  772.0 0.9 constant_dynamic-slice_fusion.26
  775.3 0.9 constant_dynamic-slice_fusion.26
  778.5 0.9 constant_dynamic-slice_fusion.26
  791.6 0.9 constant_dynamic-slice_fusion.26
  959.0 1.2 fusion.14
  960.2 1.3 exponential_reduce_fusion.9
  962.9 135.7 %all-reduce.3 = (f32[256]{0:T(256)S(1)}, f32[256]{0:T(256)S(1)}, f32[128]{0:T(128)S(1)}) all-reduce(f32[256]{0:T(256)S(1)} %fusion.9, f32[256]{0:T(256)S(1)} %fusion.4, f32[128]{0:T(128)S(1)} %fusion.14), channel_id=1, replica_groups=mesh['row'=64,'col'=8] {'col'}, use_global_device_ids=true, to_apply=%region_21.0 | all-reduce | flops 640 | bytes 5120 | tf_op jit(solution)/shard_map/pmax | solution.py:73
  1098.6 12.4 all-reduce.1
  1111.2 1.2 fusion.20
  1112.4 1.3 fusion.18
  1114.3 61.6 %all-gather.10 = f32[65536]{0:T(1024)S(1)} all-gather(f32[1024]{0:T(1024)S(1)} %fusion.15), channel_id=12, replica_groups=mesh['row'=64,'col'=8] {'row'}, dimensions={0}, use_global_device_ids=true | all-gather | bytes 266240 | tf_op jit(solution)/shard_map/all_gather | solution.py:13
  1176.7 61.4 %all-gather.11 = f32[65536]{0:T(1024)S(1)} all-gather(f32[1024]{0:T(1024)S(1)} %exponential_reduce_fusion.8), channel_id=13, replica_groups=mesh['row'=64,'col'=8] {'row'}, dimensions={0}, use_global_device_ids=true | all-gather | bytes 266240 | tf_op jit(solution)/shard_map/all_gather | solution.py:13
  1238.9 1.7 reshape.50
  1240.8 63.6 %all-gather.6 = f32[65536]{0:T(1024)S(1)} all-gather(f32[1024]{0:T(1024)S(1)} %fusion.10), channel_id=8, replica_groups=mesh['row'=64,'col'=8] {'row'}, dimensions={0}, use_global_device_ids=true | all-gather | bytes 266240 | tf_op jit(solution)/shard_map/all_gather | solution.py:13
  1304.5 63.7 %all-gather.7 = f32[65536]{0:T(1024)S(1)} all-gather(f32[1024]{0:T(1024)S(1)} %exponential_reduce_fusion.4), channel_id=9, replica_groups=mesh['row'=64,'col'=8] {'row'}, dimensions={0}, use_global_device_ids=true | all-gather | bytes 266240 | tf_op jit(solution)/shard_map/all_gather | solution.py:13
  1368.8 71.7 %all-gather.8 = f32[131072]{0:T(1024)S(1)} all-gather(f32[2048]{0:T(1024)S(1)} %fusion.5), channel_id=10, replica_groups=mesh['row'=64,'col'=8] {'row'}, dimensions={0}, use_global_device_ids=true | all-gather | bytes 532480 | tf_op jit(solution)/shard_map/all_gather | solution.py:13
  1440.6 72.6 %all-gather.9 = f32[131072]{0:T(1024)S(1)} all-gather(f32[2048]{0:T(1024)S(1)} %exponential_reduce_fusion), channel_id=11, replica_groups=mesh['row'=64,'col'=8] {'row'}, dimensions={0}, use_global_device_ids=true | all-gather | bytes 532480 | tf_op jit(solution)/shard_map/all_gather | solution.py:13
  1513.3 1.2 fusion.17
  1514.5 104.4 %while.51 = (s32[]{:T(128)}, f32[1024]{0:T(1024)S(1)}, f32[1024]{0:T(1024)S(1)}, f32[2048]{0:T(1024)S(1)}, f32[2048]{0:T(1024)S(1)}, /*index=5*/f32[1024]{0:T(10...) while((s32[]{:T(128)}, f32[1024]{0:T(1024)S(1)}, ...), condition=%wide.region_39.0_spmd, body=%wide.region_38.0_spmd.sunk | while | flops 24581 | bytes 164043 | solution.py:19
  1622.4 1.2 fusion.19
  1625.5 221.6 %all-reduce = (f32[]{:T(128)}, f32[]{:T(128)}, f32[]{:T(128)}) all-reduce(f32[]{:T(128)S(6)} %add.322, f32[]{:T(128)S(6)} %add.326, f32[]{:T(128)S(6)} %add.329), channel_id=1, replica_groups=mesh['row'=64,'col'=8] {'row','col'}, use_global_device_ids=true, to_apply=%region_42.0 | all-reduce | flops 3 | bytes 24 | tf_op jit(solution)/shard_map/psum | solution.py:108
  (972 shorter events, 315.6 us)
Async XLA Ops:
  7.2 144.3 %all-gather.15.cloned.1.call-start = ((), (), s32[]{:S(2)}) async-start(), calls=%async_computation | async-start | bytes 3194880 | tf_op jit(solution)/shard_map/all_gather | solution.py:50
  7.9 294.1 %all-gather.17.cloned.1.call-start = ((), (), s32[]{:S(2)}) async-start(), calls=%async_computation.1 | async-start | bytes 6389760 | tf_op jit(solution)/shard_map/all_gather | solution.py:49
  42.4 114.2 %copy-start.4 = (bf16[256,1536]{1,0:T(8,128)(2,1)}, bf16[256,1536]{1,0:T(8,128)(2,1)S(1)}, u32[]{:S(2)}) copy-start(bf16[256,1536]{1,0:T(8,128)(2,1)S(1)} %all_gather.84) | copy-start | bytes 2359300
  151.5 2.8 copy-start.2
  155.5 0.8 copy-start
  302.0 4.6 copy-start.3
  407.3 131.9 %copy-start.7 = (f32[65536]{0:T(1024)}, f32[65536]{0:T(1024)S(1)}, u32[]{:S(2)}) copy-start(f32[65536]{0:T(1024)S(1)} %all-gather.4) | copy-start | bytes 786436
  469.3 0.7 copy-start.8
  536.8 0.7 copy-start.9
  601.1 0.7 copy-start.10
  603.6 149.7 %slice-start.1 = ((f32[65536]{0:T(1024)}), f32[1024]{0:T(1024)S(1)}, s32[]{:S(2)}) async-start(f32[65536]{0:T(1024)} %copy-done.7), calls=%async_computation.3 | async-start | bytes 8192 | tf_op jit(solution)/shard_map/slice | solution.py:14
  603.6 149.7 %slice-start.2 = ((f32[65536]{0:T(1024)}), f32[1024]{0:T(1024)S(1)}, s32[]{:S(2)}) async-start(f32[65536]{0:T(1024)} %copy-done.8), calls=%async_computation.4 | async-start | bytes 8192 | tf_op jit(solution)/shard_map/slice | solution.py:14
  603.6 149.7 %slice-start.3 = ((f32[65536]{0:T(1024)}), f32[1024]{0:T(1024)S(1)}, s32[]{:S(2)}) async-start(f32[65536]{0:T(1024)} %copy-done.9), calls=%async_computation.5 | async-start | bytes 8192 | tf_op jit(solution)/shard_map/slice | solution.py:14
  603.6 149.7 %slice-start.4 = ((f32[65536]{0:T(1024)}), f32[1024]{0:T(1024)S(1)}, s32[]{:S(2)}) async-start(f32[65536]{0:T(1024)} %copy-done.10), calls=%async_computation.6 | async-start | bytes 8192 | tf_op jit(solution)/shard_map/slice | solution.py:14
  677.0 0.8 copy-start.5
  677.8 75.5 %slice-start = ((f32[131072]{0:T(1024)}), f32[2048]{0:T(1024)S(1)}, s32[]{:S(2)}) async-start(f32[131072]{0:T(1024)} %copy-done.5), calls=%async_computation.2 | async-start | bytes 16384 | tf_op jit(solution)/shard_map/slice | solution.py:14
  750.5 0.8 copy-start.6
  1111.0 3.0 copy-start.1
  1175.9 192.9 %copy-start.11 = (f32[65536]{0:T(1024)}, f32[65536]{0:T(1024)S(1)}, u32[]{:S(2)}) copy-start(f32[65536]{0:T(1024)S(1)} %all-gather.10) | copy-start | bytes 786436
  1238.1 0.7 copy-start.12
  1368.8 145.7 %slice-start.6 = ((f32[65536]{0:T(1024)}), f32[1024]{0:T(1024)S(1)}, s32[]{:S(2)}) async-start(f32[65536]{0:T(1024)} %copy-done.12), calls=%async_computation.8 | async-start | bytes 8192 | tf_op jit(solution)/shard_map/slice | solution.py:14
  1440.5 74.0 %slice-start.5 = ((f32[65536]{0:T(1024)}), f32[1024]{0:T(1024)S(1)}, s32[]{:S(2)}) async-start(f32[65536]{0:T(1024)} %copy-done.11), calls=%async_computation.7 | async-start | bytes 8192 | tf_op jit(solution)/shard_map/slice | solution.py:14
Sparse Core Ops, SparseCore 0:
  10.9 140.4 all-gather.14
  154.4 147.5 all-gather.16
where the time goes:
time: 1880 us; the launch traced here: 1860 us
  blocking collectives  1220 us (65%)
  local copies, waits for them, and re-layouts  319 us (17%)
  waiting for transfers between devices  254 us (14%)
  other arithmetic  27.3 us (1%)
  between operations  21.3 us (1%)
    all_gather x12, blocking collectives, combined_all(): everything = jax.tree.map(lambda part: lax.all_gather(part, axis), x)  789 us
    dynamic_slice x630, local copies, waits for them, and re-layouts, step(): return combine(so_far, jax.tree.map(lambda part: part[k], everything))  301 us
    psum x1, blocking collectives, per_device(): lax.psum((partial_values[0], partial_values[1], partial_values[2]), ('row...  222 us
    pmax x2, blocking collectives, per_device(): row_tops = lax.pmax((tops[0], tops[1], tops[2]), 'col')  156 us
    all_gather x1, waiting for transfers between devices, per_device(): lax.all_gather(earlier_vectors, 'row', axis=0, tiled=True)  144 us
    all_gather x1, waiting for transfers between devices, per_device(): lax.all_gather(later_vectors, 'row', axis=0, tiled=True)  109 us
  transfers between devices with their start and end apart: 2, of which 2 were waited for; matrix products, arithmetic and copies ran while one was open for 0% of the time, Pallas kernels for 0%

commit v1 on v0

v1 whole, which is shorter than its diff:
```python
import functools

import jax
import jax.numpy as jnp
import numpy as np
from jax import lax
from jax.experimental import pallas as pl
from jax.experimental.pallas import tpu as pltpu
from jax.sharding import PartitionSpec as P

EPSILON = 0.04
ITERS = 2
MESH = pl.DeviceIdType.MESH

NX, NY, NZ = 4, 4, 16
PLANE = NX * NY
HALF = NZ // 2
NEAR = 4
FAR = NZ // NEAR
UNIT = 16
UNITS = 3
TILE = 256
STEP = 128
SCALE = float(np.log2(np.e)) / EPSILON


def add(a, b):
    return a + b


def tree(op, parts):
    while len(parts) > 1:
        parts = [op(parts[i], parts[i + 1]) for i in range(0, len(parts) - 1, 2)] + (
            [parts[-1]] if len(parts) % 2 else []
        )
    return parts[0]


def fold_rows(x, op):
    return tree(op, [x[8 * k : 8 * k + 8] for k in range(x.shape[0] // 8)])


def each(lower, upper, body):
    def step(k, carry):
        body(k)
        return carry

    lax.fori_loop(lower, upper, step, 0)


def kernel(
    src_ref,
    tgt_ref,
    out_ref,
    rows,
    cols,
    scores,
    best,
    acc,
    acc_cross,
    pot,
    col_pot,
    phi_ref,
    totals,
    row_send,
    row_recv,
    near_send,
    near_recv,
    far_send,
    far_recv,
    sum_send,
    sum_recv,
    own_sem,
    z_rs,
    sib_rs,
    first_rs,
    second_rs,
    onward_rs,
    gather_ss,
    row_ss,
    row_rs,
    near_ss,
    near_rs,
    far_ss,
    far_rs,
    sum_ss,
    sum_rs,
):
    a, width = src_ref.shape
    b = tgt_ref.shape[0]
    n_src, n_tgt = a * PLANE * NZ * 2, b * PLANE * NZ * 2
    log_src, log_tgt = float(np.log2(n_src)), float(np.log2(n_tgt))
    rows_src, rows_tgt = a * PLANE, b * PLANE
    cols_src, cols_tgt = a * NZ * 2, b * NZ * 2
    last = cols_src + cols_tgt
    lanes_src, lanes_tgt = cols_src // 128, cols_tgt // 128
    blocks_src, blocks_tgt = rows_src // 128, rows_tgt // 128

    row, col = lax.axis_index("row"), lax.axis_index("col")
    y, z = lax.div(row, NZ), lax.rem(row, NZ)
    x, core = lax.div(col, 2), lax.rem(col, 2)
    other = 1 - core
    place = y * NX + x

    def device(xx, yy, zz, cc):
        return (yy * NZ + zz, xx * 2 + cc)

    def remote(src, dst, ss, rs, to):
        return pltpu.make_async_remote_copy(
            src_ref=src, dst_ref=dst, send_sem=ss, recv_sem=rs, device_id=to, device_id_type=MESH
        )

    def plane_peer(k):
        q = lax.rem(place + k, PLANE)
        return device(lax.rem(q, NX), lax.div(q, NX), z, core)

    z_near, z_far = lax.rem(z, NEAR), lax.div(z, NEAR)
    up, down = device(x, y, lax.rem(z + 1, NZ), core), device(x, y, lax.rem(z + NZ - 1, NZ), core)

    def arrived(sem, at):
        remote(at, at, sem, sem, up).wait_recv()

    def gone(sem, at):
        remote(at, at, sem, sem, up).wait_send()

    barrier = pltpu.get_barrier_semaphore()
    greeted = [
        up,
        down,
        device(x, y, z, other),
        device(lax.rem(x + 1, NX), y, z, core),
        device(lax.rem(x + NX - 1, NX), y, z, core),
        device(x, lax.rem(y + 1, NY), z, core),
        device(x, lax.rem(y + NY - 1, NY), z, core),
    ]
    for to in greeted:
        pl.semaphore_signal(barrier, inc=1, device_id=to, device_id_type=MESH)

    MIDDLE = HALF - 1

    def src_start(pos, at_last, c):
        usual = 2 * a * pos
        return pl.multiple_of(usual + at_last * (last + 2 * a - usual) + a * c, UNIT)

    def tgt_start(pos, at_last, c):
        quarter = lax.div(pos + NZ // 4, NZ // 2)
        stored = pos + quarter * (12 - 8 * quarter) * (NZ // 16)
        usual = cols_src + 2 * b * stored
        return pl.multiple_of(usual + at_last * (last - usual) + b * c, UNIT)

    def unit_start(pos, at_last, u):
        if u == 2:
            return tgt_start(pos, at_last, core)
        return pl.multiple_of(src_start(pos, at_last, core) + UNIT * u, UNIT)

    def z_copy(flow, step, u):
        way = 1 - 2 * flow
        at = (flow * HALF + step - 1) * UNITS + u
        before = unit_start(MIDDLE + way * (step - 1), 0, u)
        after = unit_start(MIDDLE + way * step, lax.div(step, HALF), u)
        return remote(
            cols.at[pl.ds(before, UNIT), pl.ds(0, width)],
            cols.at[pl.ds(after, UNIT), pl.ds(0, width)],
            gather_ss.at[0],
            z_rs.at[at],
            up if flow else down,
        )

    def sib_send(step, pos):
        at_last = lax.div(step, HALF)
        sem = lax.div(step + 3, HALF) + at_last
        for start, size in ((src_start(pos, at_last, core), a), (tgt_start(pos, at_last, core), b)):
            at = cols.at[pl.ds(start, size)]
            remote(at, at, gather_ss.at[1], sib_rs.at[sem], device(x, y, z, other)).start()

    def sib_wait(sem, slots):
        arrived(sib_rs.at[sem], cols.at[pl.ds(0, slots * (a + b))])

    def shifted(u, first, second):
        later = lax.div(u * (u - 1), 2)
        f = lax.div((1 - u) * (2 - u), 2) + later * (1 - core)
        xx = lax.rem(x + f * first + (1 - f) * second, NX)
        yy = lax.rem(y + f * second + (1 - f) * first, NY)
        q = yy * NX + xx
        start = (a - (a - b) * later) * q + UNIT * u * (1 - later) + rows_src * later
        return device(xx, yy, z, core), rows.at[pl.ds(pl.multiple_of(start, UNIT), UNIT)]

    def plane_copy(at, sem, to):
        return remote(at, at, gather_ss.at[2], sem, to)

    def first_send(u, k):
        plane_copy(shifted(u, 0, 0)[1], first_rs.at[4 * u + k], shifted(u, k, 0)[0]).start()

    def first_arrival(u, k):
        arrived(first_rs.at[4 * u + k], shifted(u, 4 - k, 0)[1])

    def first_onward(u):
        way = 1 + 2 * lax.rem(u, 2)
        plane_copy(shifted(u, 4 - way, 0)[1], first_rs.at[4 * u + 2], shifted(u, way, 0)[0]).start()

    def second_sends(u, j):
        for k in (1, 3):
            sem = second_rs.at[4 * (4 * u + j) + k]
            plane_copy(shifted(u, 4 - j, 0)[1], sem, shifted(u, 0, k)[0]).start()

    def second_onward(u, j):
        for k in (1, 3):
            arrived(second_rs.at[4 * (4 * u + j) + k], shifted(u, 4 - j, 4 - k)[1])
        way = 1 + 2 * lax.rem(j, 2)
        plane_copy(shifted(u, 4 - j, 4 - way)[1], onward_rs.at[0], shifted(u, 0, way)[0]).start()

    def norm_lanes(source, start, size, targets):
        lane_own = lax.broadcasted_iota(jnp.int32, (size, 128), 1)
        v = source[pl.ds(start, size), 0:width].astype(jnp.float32)
        v = v * v
        total = tree(add, [v[:, 128 * h : 128 * h + 128] for h in range(width // 128)])
        rest = -0.5 * jnp.sum(total, axis=1, keepdims=True)
        terms = []
        for _ in range(3):
            term = rest.astype(jnp.bfloat16).astype(jnp.float32)
            rest = rest - term
            terms.append(term)
        for target, at, first in targets:
            more = jnp.where(lane_own < 6, 1.0, 0.0)
            for k, term in enumerate(terms):
                more = jnp.where(lane_own == first + k, term, more)
            target[pl.ds(at, size), width : width + 128] = more.astype(jnp.bfloat16)

    mine = (
        (src_ref, a, pl.multiple_of(a * place, UNIT), src_start(MIDDLE, 0, core)),
        (tgt_ref, b, pl.multiple_of(rows_src + b * place, UNIT), tgt_start(MIDDLE, 0, core)),
    )
    own_copies = []
    for kind, (ref, size, as_row, as_col) in enumerate(mine):
        for k, (target, at) in enumerate(((rows, as_row), (cols, as_col))):
            own_copies.append(
                pltpu.make_async_copy(
                    ref, target.at[pl.ds(at, size), pl.ds(0, width)], own_sem.at[2 * kind + k]
                )
            )
    for copy in own_copies:
        copy.start()
    row_recv[...] = jnp.ones(row_recv.shape, jnp.float32)
    row_send[...] = jnp.ones(row_send.shape, jnp.float32)
    for copy in own_copies:
        copy.wait()
    pl.semaphore_wait(barrier, len(greeted))

    for u in range(UNITS):
        z_copy(0, 1, u).start()
        z_copy(1, 1, u).start()
    for _, size, as_row, as_col in mine:
        norm_lanes(rows, as_row, size, [(rows, as_row, 0), (cols, as_col, 3)])

    def plane_start(u):
        first_send(u, 1)
        first_send(u, 3)

    each(0, UNITS, plane_start)
    each(0, UNITS, lambda u: second_sends(u, 0))
    sib_send(0, MIDDLE)

    outer_end = cols_src + cols_tgt // 2
    empty = jnp.zeros((2 * a, width + 128), jnp.bfloat16)
    cols[cols_src - 2 * a : cols_src, :] = empty
    cols[outer_end - 2 * b : outer_end, :] = empty[: 2 * b]
    cols[last + 2 * b : last + 2 * a, :] = empty[: 2 * a - 2 * b]

    def product(r, start, size):
        at = pl.ds(pl.multiple_of(r * TILE, TILE), TILE)
        cross = lax.dot_general(
            rows[at, :],
            cols[pl.ds(pl.multiple_of(start, 128), size), :],
            (((1,), (1,)), ((), ())),
            preferred_element_type=jnp.float32,
        )
        return at, [cross[:, 128 * h : 128 * h + 128] * SCALE for h in range(size // 128)]

    def tile(t):
        outer, i = lax.div(t, 7), lax.rem(t, 7)
        is_tgt = lax.div(i, 4)
        r = lax.rem(i, 2) + 2 * lax.div(i, 6)
        g = (1 - outer) * (1 + lax.div(i, 2)) + outer * 3 * lax.div(i, 2)
        at, (one, two) = product(
            r, (1 - is_tgt) * TILE * g + is_tgt * (cols_src + (1 - outer) * (cols_tgt // 2)), TILE
        )
        is_self = (i < 4) | (i == 6)
        lane_one = (1 - is_tgt) * TILE * g + is_tgt * (cols_src + 128 * (1 - outer))
        lane_two = (1 - is_tgt) * (TILE * g + 128) + is_tgt * (cols_src + 256 + 128 * outer)
        for value, lanes in ((one, lane_one), (two, lane_two)):
            scores[at, pl.ds(pl.multiple_of(lanes, 128), 128)] = jnp.where(is_self, jnp.exp2(value), value)

    lane1 = lax.broadcasted_iota(jnp.int32, (1, 128), 1)

    def last_tile(r):
        at, (value,) = product(r, last, 128)
        e = jnp.exp2(value)
        src_lanes, tgt_lanes = slice(cols_src - 128, cols_src), slice(last - 128, last)
        scores[at, src_lanes] = jnp.where(lane1 >= 2 * a, e, scores[at, src_lanes])
        moved = pltpu.roll(jnp.where(r * TILE < rows_src, value, e), 128 - 2 * b, 1)
        scores[at, tgt_lanes] = jnp.where(lane1 >= 128 - 2 * b, moved, scores[at, tgt_lanes])

    def ring_step(step):
        for u in range(UNITS):
            for flow in range(2):
                steps = HALF if flow == (1 if u == 1 else 0) else HALF - 1

                @pl.when(step <= steps)
                def _():
                    z_copy(flow, step, u).wait_recv()

                @pl.when(step < steps)
                def _():
                    z_copy(flow, step + 1, u).start()

        def to_other(flow):
            pos = MIDDLE + (1 - 2 * flow) * step
            at_last = lax.div(step, HALF)
            for start, size in ((src_start(pos, at_last, core), a), (tgt_start(pos, at_last, core), b)):
                norm_lanes(cols, start, size, [(cols, start, 3)])
            sib_send(step, pos)

        each(0, 2 - lax.div(step, HALF), to_other)

        @pl.when(step == 1)
        def _():
            def stage(u):
                first_arrival(u, 1)
                first_arrival(u, 3)
                first_onward(u)
                second_sends(u, 1)
                second_sends(u, 3)

            each(0, UNITS, stage)

        @pl.when(step == 2)
        def _():
            def stage(u):
                first_arrival(u, 2)
                second_sends(u, 2)

            each(0, UNITS, stage)

        @pl.when((step >= 2) & (step <= 4))
        def _():
            def stage(i):
                u, k = lax.rem(i, UNITS), lax.div(i, UNITS)
                second_onward(u, k + lax.div(k, 2) - 2 * lax.div(k, 3))

            each(
                UNITS * (2 * step - 4 - lax.div(step, 3)),
                UNITS * (2 * step - 3 - lax.div(step, 4)),
                stage,
            )

        @pl.when(step == 5)
        def _():
            arrived(onward_rs.at[0], rows.at[pl.ds(0, 4 * UNITS * UNIT)])
            sib_wait(0, 9)

        @pl.when(step == 7)
        def _():
            sib_wait(1, 6)

        @pl.when(step >= 5)
        def _():
            each(lax.div(7 * (step - 5) + 1, 2), lax.div(7 * (step - 4) + 1, 2), tile)

    each(1, HALF + 1, ring_step)
    sib_wait(2, 1)
    each(0, (rows_src + rows_tgt) // TILE, last_tile)

    lane = lax.broadcasted_iota(jnp.int32, (128, 128), 1)
    lane8 = lax.broadcasted_iota(jnp.int32, (8, 128), 1)
    sub8 = lax.broadcasted_iota(jnp.int32, (8, 128), 0)
    sub16 = lax.broadcasted_iota(jnp.int32, (16, 128), 0)
    used_rows = 2 * blocks_src + blocks_tgt
    is_cross = sub16 < blocks_src
    row_log = jnp.where((sub16 >= blocks_src) & (sub16 < 2 * blocks_src), log_src, log_tgt)

    def over_rows(count, body, init):
        return lax.fori_loop(0, count // STEP, lambda r, c: body(pl.multiple_of(r * STEP, STEP), c), init)

    def zeros8(count):
        return tuple(jnp.zeros((8, 128), jnp.float32) for _ in range(count))

    def roll_flat(block, lanes, rows_on):
        rolled = pltpu.roll(block, lanes, 1)
        rolled = jnp.where(lane8 < lanes, pltpu.roll(rolled, 1, 0), rolled)
        return pltpu.roll(rolled, rows_on, 0)

    def turned(earlier, both, chips):
        flat = 2 * a * chips
        earlier = roll_flat(earlier, lax.rem(flat, 128), lax.div(flat, 128))
        flat = 2 * b * chips
        lanes, rows_on = lax.rem(flat, 128), lax.div(flat, 128)
        swapped = pltpu.roll(both, 4, 0)
        cross = roll_flat(jnp.where(sub8 < 4, both, swapped), lanes, rows_on)
        later = roll_flat(jnp.where(sub8 < 4, swapped, both), lanes, rows_on)
        return earlier, jnp.where(sub8 < 4, cross, later)

    chips_on = lax.rem(z + HALF + 1, NZ)

    def merged(parts, logs):
        total = tree(add, parts)
        if logs is None:
            return total
        top = tree(jnp.maximum, parts)
        return jnp.where((sub8 < 4) & logs, top + jnp.log2(tree(add, [jnp.exp2(p - top) for p in parts])), total)

    def lanes_at(h, first=0):
        return slice(first + 128 * h, first + 128 * h + 128)

    col_pot[0] = jnp.ones((8, 128), jnp.float32)
    col_pot[1] = jnp.where(sub8 < 4, 0.0, 1.0)

    def iteration(index):
        def src_rows_part(r):
            at = pl.ds(r, 32)
            values = [scores[at, lanes_at(h, cols_src)] + col_pot[1, h : h + 1] for h in range(lanes_tgt)]
            top = tree(jnp.maximum, values)
            best[at, :] = top
            acc_cross[at, :] = tree(add, [jnp.exp2(v - top) for v in values])
            acc[at, :] = tree(add, [scores[at, lanes_at(h)] * col_pot[0, h : h + 1] for h in range(lanes_src)])

        def tgt_rows_part(r):
            at = pl.ds(rows_src + r, 32)
            acc[at, :] = tree(
                add,
                [scores[at, lanes_at(h, cols_src)] * col_pot[1, 4 + h : 5 + h] for h in range(lanes_tgt)],
            )

        def in_parts(part):
            def body(r, carry):
                for k in range(STEP // 32):
                    part(r + 32 * k)
                return carry

            return body

        over_rows(rows_src, in_parts(src_rows_part), 0)
        over_rows(rows_tgt, in_parts(tgt_rows_part), 0)
        def over_sublanes(block, op, reduce):
            return reduce(fold_rows(block, op), axis=0, keepdims=True)

        for r in range(blocks_src + blocks_tgt):
            at = slice(128 * r, 128 * r + 128)
            if r < blocks_src:
                each_top = best[at, :].T
                top = over_sublanes(each_top, jnp.maximum, jnp.max)
                total = over_sublanes(acc_cross[at, :].T * jnp.exp2(each_top - top), add, jnp.sum)
                row_send[index, r : r + 1] = top + jnp.log2(total)
            row = blocks_src + r
            row_send[index, row : row + 1] = over_sublanes(acc[at, :].T, add, jnp.sum)
        row_recv[index, place] = row_send[index]
        sent = row_send.at[index, pl.ds(0, used_rows)]
        for k in range(1, PLANE):
            remote(
                sent,
                row_recv.at[index, place, pl.ds(0, used_rows)],
                row_ss.at[index],
                row_rs.at[index],
                plane_peer(k),
            ).start()
        others = row_recv.at[index, pl.ds(0, PLANE - 1), pl.ds(0, used_rows)]
        arrived(row_rs.at[index], others)
        parts = [row_recv[index, q] for q in range(PLANE)]
        top = tree(jnp.maximum, parts)
        spread = top + jnp.log2(tree(add, [jnp.exp2(p - top) for p in parts]))
        phi = row_log - jnp.where(is_cross, spread, jnp.log2(tree(add, parts)))
        phi_ref[...] = phi
        table = jnp.where(is_cross, phi, jnp.exp2(phi))
        table = jnp.concatenate([table, jnp.zeros((112, 128), jnp.float32)], axis=0).T
        for r in range(used_rows):
            pot[128 * r : 128 * r + 128, :] = jnp.broadcast_to(table[:, r : r + 1], (128, 128))

        def weighted_cols(first_row, first_col, first_pot, count, lanes):
            def body(r, sums):
                w = pot[pl.ds(first_pot + r, STEP), :]
                return tuple(
                    sums[h] + fold_rows(scores[pl.ds(first_row + r, STEP), lanes_at(h, first_col)] * w, add)
                    for h in range(lanes)
                )

            sums = over_rows(count, body, zeros8(lanes))
            return [jnp.sum(s, axis=0, keepdims=True) for s in sums]

        def cross_body(r, carry):
            w = pot[pl.ds(r, STEP), :]
            out = []
            for h in range(lanes_tgt):
                values = scores[pl.ds(r, STEP), lanes_at(h, cols_src)] + w
                top, total = carry[2 * h], carry[2 * h + 1]
                new_top = jnp.maximum(top, fold_rows(values, jnp.maximum))
                parts = [jnp.exp2(values[8 * k : 8 * k + 8] - new_top) for k in range(STEP // 8)]
                out += [new_top, total * jnp.exp2(top - new_top) + tree(add, parts)]
            return tuple(out)

        start = (jnp.full((8, 128), -1e30, jnp.float32), jnp.zeros((8, 128), jnp.float32))
        sums = over_rows(rows_src, cross_body, start * lanes_tgt)
        tops = [jnp.max(t, axis=0, keepdims=True) for t in sums[::2]]
        sums = [t * jnp.exp2(m - top) for t, m, top in zip(sums[1::2], sums[::2], tops)]
        both = [tops[h] + jnp.log2(jnp.sum(sums[h], axis=0, keepdims=True)) for h in range(lanes_tgt)]
        both = both + weighted_cols(rows_src, cols_src, 2 * rows_src, rows_tgt, lanes_tgt)
        earlier = weighted_cols(0, 0, rows_src, rows_src, lanes_src)
        blocks = turned(jnp.concatenate(earlier, axis=0), jnp.concatenate(both, axis=0), chips_on)
        weight = jnp.where(
            is_cross,
            1.0 / (n_src * SCALE),
            jnp.where(
                sub16 < 2 * blocks_src,
                -0.5 / (n_src * SCALE),
                jnp.where(sub16 < used_rows, -0.5 / (n_tgt * SCALE), 0.0),
            ),
        )
        extra = jnp.sum(phi * weight, axis=0, keepdims=True)

        size = 9
        me_near = 2 * z_near + core
        for k in range(2):
            near_send[index, k, 0:8] = blocks[k]
            near_send[index, k, 8:9] = jnp.zeros_like(extra) if k else extra
        near_recv[index, me_near] = near_send[index, core]

        def near_send_to(o):
            zn, cc = lax.rem(z_near + o // 2, NEAR), lax.rem(core + o % 2, 2)
            remote(
                near_send.at[index, cc, pl.ds(0, size)],
                near_recv.at[index, me_near, pl.ds(0, size)],
                near_ss.at[index],
                near_rs.at[index],
                device(x, y, NEAR * z_far + zn, cc),
            ).start()

        for o in range(1, 2 * NEAR):
            near_send_to(o)
        others = near_recv.at[index, pl.ds(0, 2 * NEAR - 1), pl.ds(0, size)]
        arrived(near_rs.at[index], others)
        me_far = 2 * z_far + core
        block = merged([near_recv[index, q, 0:8] for q in range(2 * NEAR)], core == 1)
        extra = tree(add, [near_recv[index, q, 8:9] for q in range(2 * NEAR)])
        far_send[index, 0:8] = block
        far_send[index, 8:9] = extra
        far_recv[index, me_far, 0:8] = block
        far_recv[index, me_far, 8:9] = extra

        def far_send_to(o):
            zf, cc = lax.rem(z_far + o // 2, FAR), lax.rem(core + o % 2, 2)
            remote(
                far_send.at[index, pl.ds(0, size)],
                far_recv.at[index, me_far, pl.ds(0, size)],
                far_ss.at[index],
                far_rs.at[index],
                device(x, y, NEAR * zf + z_near, cc),
            ).start()

        for o in range(1, 2 * FAR):
            far_send_to(o)
        others = far_recv.at[index, pl.ds(0, 2 * FAR - 1), pl.ds(0, size)]
        arrived(far_rs.at[index], others)
        earlier = merged([far_recv[index, 2 * q, 0:8] for q in range(FAR)], None)
        both = merged([far_recv[index, 2 * q + 1, 0:8] for q in range(FAR)], True)
        totals[0] = earlier
        totals[1] = both
        totals[2, 0:1] = tree(add, [far_recv[index, 2 * q, 8:9] for q in range(FAR)])

        @pl.when(index == 0)
        def _():
            earlier_pot, both_pot = turned(
                n_src / earlier,
                jnp.where(sub8 < 4, log_src - both, n_tgt / both),
                lax.rem(NZ - chips_on, NZ),
            )
            col_pot[0] = earlier_pot
            col_pot[1] = both_pot

    each(0, ITERS, iteration)

    earlier, both = totals[0], totals[1]
    both = (1.0 / SCALE) * jnp.where(sub8 < 4, log_src - both, log_tgt - jnp.log2(both))
    earlier = (1.0 / SCALE) * (log_src - jnp.log2(earlier))
    share = jnp.where(sub8 < 4, 1.0 / n_tgt, -0.5 / n_tgt) * both - (0.5 / n_src) * earlier
    share = jnp.sum(share, axis=0, keepdims=True)

    sum_send[...] = share
    sum_recv[place] = share
    for k in range(1, PLANE):
        remote(sum_send, sum_recv.at[place], sum_ss.at[0], sum_rs.at[0], plane_peer(k)).start()

    def front(block, at, size):
        per = 128 // size
        return pltpu.roll(
            pltpu.roll(block, lax.rem(8 - lax.div(at, per), 8), 0),
            lax.rem(128 - size * lax.rem(at, per), 128),
            1,
        )

    duals = phi_ref[...] * (1.0 / SCALE)
    src_rows = front(duals[0:8], place, a)
    tgt_rows = front(duals[8:16], place, b)
    tgt_cols = front(both, 2 * z + core, b)
    returned = jnp.where(
        sub8 == 1,
        pltpu.roll(src_rows, 5, 0),
        jnp.where(
            sub8 == 2,
            pltpu.roll(tgt_rows, 2, 0),
            jnp.where(sub8 == 3, pltpu.roll(tgt_cols, 3, 0), src_rows),
        ),
    )
    gone(gather_ss.at[0], cols.at[pl.ds(0, UNIT * (2 * HALF - 1) * UNITS), pl.ds(0, width)])
    gone(gather_ss.at[1], cols.at[pl.ds(0, NZ * (a + b))])
    gone(gather_ss.at[2], rows.at[pl.ds(0, UNIT * (PLANE - 1) * UNITS)])
    for index in range(ITERS):
        gone(row_ss.at[index], row_recv.at[index, pl.ds(0, PLANE - 1), pl.ds(0, used_rows)])
        gone(near_ss.at[index], near_recv.at[index, pl.ds(0, 2 * NEAR - 1), pl.ds(0, 9)])
        gone(far_ss.at[index], far_recv.at[index, pl.ds(0, 2 * FAR - 1), pl.ds(0, 9)])
    others = sum_recv.at[pl.ds(0, PLANE - 1)]
    arrived(sum_rs.at[0], others)
    share = totals[2, 0:1] + tree(add, [sum_recv[q] for q in range(PLANE)])
    out_ref[...] = jnp.where(sub8 == 4, jnp.sum(share, axis=1, keepdims=True), returned)
    gone(sum_ss.at[0], others)


def hand_out(block_ref, left_ref, right_ref, earlier_ref, later_ref, div_ref):
    for k, ref in enumerate((left_ref, earlier_ref, later_ref, right_ref, div_ref)):
        ref[...] = block_ref[k : k + 1, 0 : ref.shape[1]]


def per_device(earlier_vectors, later_vectors):
    a, width = earlier_vectors.shape
    b = later_vectors.shape[0]
    rows_src, rows_tgt = a * PLANE, b * PLANE
    cols_src, cols_tgt = 2 * a * NZ, 2 * b * NZ
    rows_all, cols_all = rows_src + rows_tgt, cols_src + cols_tgt
    f32, bf16 = jnp.float32, jnp.bfloat16
    dma = pltpu.SemaphoreType.DMA
    wide = width + 128
    block = pl.pallas_call(
        kernel,
        out_shape=jax.ShapeDtypeStruct((8, 128), f32),
        in_specs=[pl.BlockSpec(memory_space=pltpu.HBM)] * 2,
        out_specs=pl.BlockSpec(memory_space=pltpu.VMEM),
        scratch_shapes=[
            pltpu.VMEM((rows_all, wide), bf16),
            pltpu.VMEM((cols_all + 128, wide), bf16),
            pltpu.VMEM((rows_all, cols_all), f32),
            pltpu.VMEM((rows_src, 128), f32),
            pltpu.VMEM((rows_all, 128), f32),
            pltpu.VMEM((rows_src, 128), f32),
            pltpu.VMEM((2 * rows_src + rows_tgt, 128), f32),
            pltpu.VMEM((2, 8, 128), f32),
            pltpu.VMEM((16, 128), f32),
            pltpu.VMEM((3, 8, 128), f32),
            pltpu.VMEM((ITERS, 16, 128), f32),
            pltpu.VMEM((ITERS, PLANE, 16, 128), f32),
            pltpu.VMEM((ITERS, 2, 16, 128), f32),
            pltpu.VMEM((ITERS, 2 * NEAR, 16, 128), f32),
            pltpu.VMEM((ITERS, 16, 128), f32),
            pltpu.VMEM((ITERS, 2 * FAR, 16, 128), f32),
            pltpu.VMEM((1, 128), f32),
            pltpu.VMEM((PLANE, 1, 128), f32),
            dma((4,)),
            dma((2 * HALF * UNITS,)),
            dma((3,)),
            dma((4 * UNITS,)),
            dma((16 * UNITS,)),
            dma((1,)),
            dma((3,)),
            dma((ITERS,)),
            dma((ITERS,)),
            dma((ITERS,)),
            dma((ITERS,)),
            dma((ITERS,)),
            dma((ITERS,)),
            dma((1,)),
            dma((1,)),
        ],
        compiler_params=pltpu.CompilerParams(
            collective_id=0, has_side_effects=True, vmem_limit_bytes=60 * 1024 * 1024
        ),
        cost_estimate=pl.CostEstimate(
            flops=2 * wide * (rows_src * cols_all + rows_tgt * cols_tgt),
            bytes_accessed=2 * width * (a + b),
            transcendentals=rows_src * (cols_src + 3 * cols_tgt) + rows_tgt * cols_tgt,
        ),
    )(earlier_vectors, later_vectors)
    vmem = pl.BlockSpec(memory_space=pltpu.VMEM)
    left, right, earlier, later, div = pl.pallas_call(
        hand_out,
        out_shape=tuple(jax.ShapeDtypeStruct(s, f32) for s in ((1, a), (1, b), (1, a), (1, b), (1, 1))),
        in_specs=[vmem],
        out_specs=(vmem,) * 5,
    )(block)
    return left.reshape(a), right.reshape(b), earlier.reshape(a), later.reshape(b), div.reshape(())


def solution(mesh):
    return jax.shard_map(
        per_device,
        mesh=mesh,
        in_specs=(P(("row", "col"), None), P(("row", "col"), None)),
        out_specs=(P(("row", "col")), P(("row", "col")), P(("row", "col")), P(("row", "col")), P()),
        check_vma=False,
    )
```

time: 1880 us -> 92.3 us (0.05); the launches traced: 1860 us -> 92.2 us
  blocking collectives: 1220 us -> 0 us
  local copies, waits for them, and re-layouts: 319 us -> 0 us
  waiting for transfers between devices: 254 us -> 0 us
  Pallas kernels: 0 us -> 91.5 us
  other arithmetic: 27.3 us -> 0 us
  between operations: 21.3 us -> 0.64 us
    all_gather x14 -> x0, blocking collectives: 822 us -> none  [the longest x12 789 us: combined_all(): everything = jax.tree.map(lambda part: lax.all_gather(part, axis), x)]
    dynamic_slice x630 -> x0, local copies, waits for them, and re-layouts: 301 us -> none  [step(): return combine(so_far, jax.tree.map(lambda part: part[k], everything))]
    all_gather x2 -> x0, waiting for transfers between devices: 253 us -> none  [the longest x1 144 us: per_device(): lax.all_gather(earlier_vectors, 'row', axis=0, tiled=True)]
    psum x3 -> x0, blocking collectives: 246 us -> none  [the longest x1 222 us: per_device(): lax.psum((partial_values[0], partial_values[1], partial_values[2]), ('row...]
    pmax x2 -> x0, blocking collectives: 156 us -> none  [per_device(): row_tops = lax.pmax((tops[0], tops[1], tops[2]), 'col')]
    pallas_call x0 -> x2, Pallas kernels: none -> 91.5 us  [the longest x1 90.3 us: per_device(): pl.pallas_call(kernel, out_shape=jax.ShapeDtypeStruct((8, 128), f32), in_...]
  transfers between devices with their start and end apart: 2 -> 0, of which waited for: 2 -> 0; matrix products, arithmetic and copies ran while one was open for 0% -> 0% of each run, Pallas kernels for 0% -> 0%
where the time goes in v1:
time: 92.3 us; the launch traced here: 92.2 us
  Pallas kernels  91.5 us (99%)
    pallas_call x1, Pallas kernels, per_device(): pl.pallas_call(kernel, out_shape=jax.ShapeDtypeStruct((8, 128), f32), in_...  90.3 us

profile of v1, /device:TPU:1, one launch (start us, length us, event | category | flops | bytes accessed | tf_op | source)
XLA Modules:
  0.0 92.2 jit_solution(12439378846351874376)
XLA Ops:
  0.6 90.3 %shard_map.65.block_ref = f32[8,128]{1,0:T(8,128)} custom-call(bf16[32,1536]{1,0:T(8,128)(2,1)} %src_ref.1, bf16[16,1536]{1,0:T(8,128)(2,1)} %tgt_ref.1), custom_call_target="tpu_custom_call" | custom-call | flops 3053453312 | bytes 147456 | tf_op jit(solution)/shard_map/pallas_call | solution.py:639
  91.0 1.2 %shard_map.66 = (f32[1,32]{1,0:T(1,128)}, f32[1,16]{1,0:T(1,128)}, f32[1,32]{1,0:T(1,128)}, f32[1,16]{1,0:T(1,128)}, f32[1,1]{1,0:T(1,128)}) custom-call(f32[8,128]{1,0:T(8,128)} %shard_map.65.block_ref), custom_call_target="tpu_custom_call" | custom-call | tf_op jit(solution)/shard_map/pallas_call | solution.py:689

commit v2 on v1

--- a/solution.py
+++ b/solution.py
@@ -38,6 +38,14 @@
 
 def fold_rows(x, op):
     return tree(op, [x[8 * k : 8 * k + 8] for k in range(x.shape[0] // 8)])
+
+
+def quotient(number, by):
+    return number // by if isinstance(number, int) else lax.div(number, by)
+
+
+def multiple(number, of):
+    return number if isinstance(number, int) else pl.multiple_of(number, of)
 
 
 def each(lower, upper, body):
@@ -267,20 +275,20 @@
     cols[last + 2 * b : last + 2 * a, :] = empty[: 2 * a - 2 * b]
 
     def product(r, start, size):
-        at = pl.ds(pl.multiple_of(r * TILE, TILE), TILE)
+        at = pl.ds(multiple(r * TILE, TILE), TILE)
         cross = lax.dot_general(
             rows[at, :],
-            cols[pl.ds(pl.multiple_of(start, 128), size), :],
+            cols[pl.ds(multiple(start, 128), size), :],
             (((1,), (1,)), ((), ())),
             preferred_element_type=jnp.float32,
         )
         return at, [cross[:, 128 * h : 128 * h + 128] * SCALE for h in range(size // 128)]
 
     def tile(t):
-        outer, i = lax.div(t, 7), lax.rem(t, 7)
-        is_tgt = lax.div(i, 4)
-        r = lax.rem(i, 2) + 2 * lax.div(i, 6)
-        g = (1 - outer) * (1 + lax.div(i, 2)) + outer * 3 * lax.div(i, 2)
+        outer, i = quotient(t, 7), t - 7 * quotient(t, 7)
+        is_tgt, pair = quotient(i, 4), quotient(i, 2)
+        r = i - 2 * pair + 2 * quotient(i, 6)
+        g = (1 - outer) * (1 + pair) + outer * 3 * pair
         at, (one, two) = product(
             r, (1 - is_tgt) * TILE * g + is_tgt * (cols_src + (1 - outer) * (cols_tgt // 2)), TILE
         )
@@ -288,7 +296,11 @@
         lane_one = (1 - is_tgt) * TILE * g + is_tgt * (cols_src + 128 * (1 - outer))
         lane_two = (1 - is_tgt) * (TILE * g + 128) + is_tgt * (cols_src + 256 + 128 * outer)
         for value, lanes in ((one, lane_one), (two, lane_two)):
-            scores[at, pl.ds(pl.multiple_of(lanes, 128), 128)] = jnp.where(is_self, jnp.exp2(value), value)
+            if isinstance(t, int):
+                value = jnp.exp2(value) if is_self else value
+            else:
+                value = jnp.where(is_self, jnp.exp2(value), value)
+            scores[at, pl.ds(multiple(lanes, 128), 128)] = value
 
     lane1 = lax.broadcasted_iota(jnp.int32, (1, 128), 1)
 
@@ -297,13 +309,14 @@
         e = jnp.exp2(value)
         src_lanes, tgt_lanes = slice(cols_src - 128, cols_src), slice(last - 128, last)
         scores[at, src_lanes] = jnp.where(lane1 >= 2 * a, e, scores[at, src_lanes])
-        moved = pltpu.roll(jnp.where(r * TILE < rows_src, value, e), 128 - 2 * b, 1)
+        moved = pltpu.roll(value if r * TILE < rows_src else e, 128 - 2 * b, 1)
         scores[at, tgt_lanes] = jnp.where(lane1 >= 128 - 2 * b, moved, scores[at, tgt_lanes])
 
     def ring_step(step):
         for u in range(UNITS):
             for flow in range(2):
-                steps = HALF if flow == (1 if u == 1 else 0) else HALF - 1
+                longer = 1 if flow == (1 if u == 1 else 0) else 0
+                steps = HALF - 1 + longer + core * (1 - 2 * longer)
 
                 @pl.when(step <= steps)
                 def _():
@@ -362,13 +375,16 @@
         def _():
             sib_wait(1, 6)
 
-        @pl.when(step >= 5)
+        @pl.when((step >= 5) & (step < HALF))
         def _():
             each(lax.div(7 * (step - 5) + 1, 2), lax.div(7 * (step - 4) + 1, 2), tile)
 
     each(1, HALF + 1, ring_step)
+    for t in (11, 12, 13):
+        tile(t)
     sib_wait(2, 1)
-    each(0, (rows_src + rows_tgt) // TILE, last_tile)
+    for r in range((rows_src + rows_tgt) // TILE):
+        last_tile(r)
 
     lane = lax.broadcasted_iota(jnp.int32, (128, 128), 1)
     lane8 = lax.broadcasted_iota(jnp.int32, (8, 128), 1)

time: 92.3 us -> 92.1 us (level)
  no operation moved by 1% of the time
where the time goes in v2:
time: 92.1 us; the launch traced here: 91.9 us
  Pallas kernels  91.3 us (99%)
    pallas_call x1, Pallas kernels, per_device(): pl.pallas_call(kernel, out_shape=jax.ShapeDtypeStruct((8, 128), f32), in_...  90.1 us

profile of v2, /device:TPU:1, one launch (start us, length us, event | category | flops | bytes accessed | tf_op | source)
XLA Modules:
  0.0 91.9 jit_solution(846695498812946761)
XLA Ops:
  0.6 90.1 %shard_map.65.block_ref = f32[8,128]{1,0:T(8,128)} custom-call(bf16[32,1536]{1,0:T(8,128)(2,1)} %src_ref.1, bf16[16,1536]{1,0:T(8,128)(2,1)} %tgt_ref.1), custom_call_target="tpu_custom_call" | custom-call | flops 3053453312 | bytes 147456 | tf_op jit(solution)/shard_map/pallas_call | solution.py:655
  90.7 1.2 %shard_map.66 = (f32[1,32]{1,0:T(1,128)}, f32[1,16]{1,0:T(1,128)}, f32[1,32]{1,0:T(1,128)}, f32[1,16]{1,0:T(1,128)}, f32[1,1]{1,0:T(1,128)}) custom-call(f32[8,128]{1,0:T(8,128)} %shard_map.65.block_ref), custom_call_target="tpu_custom_call" | custom-call | tf_op jit(solution)/shard_map/pallas_call | solution.py:705

commit v3 on v2

--- a/solution.py
+++ b/solution.py
@@ -395,7 +395,9 @@
     row_log = jnp.where((sub16 >= blocks_src) & (sub16 < 2 * blocks_src), log_src, log_tgt)
 
     def over_rows(count, body, init):
-        return lax.fori_loop(0, count // STEP, lambda r, c: body(pl.multiple_of(r * STEP, STEP), c), init)
+        for r in range(0, count, STEP):
+            init = body(r, init)
+        return init
 
     def zeros8(count):
         return tuple(jnp.zeros((8, 128), jnp.float32) for _ in range(count))

time: 92.1 us -> 91.1 us (0.989)
  Pallas kernels: 91.3 us -> 90.3 us
    pallas_call x1, Pallas kernels: 90.1 us -> 89.1 us  [per_device(): pl.pallas_call(kernel, out_shape=jax.ShapeDtypeStruct((8, 128), f32), in_...]
where the time goes in v3:
time: 91.1 us; the launch traced here: 90.9 us
  Pallas kernels  90.3 us (99%)
    pallas_call x1, Pallas kernels, per_device(): pl.pallas_call(kernel, out_shape=jax.ShapeDtypeStruct((8, 128), f32), in_...  89.1 us

profile of v3, /device:TPU:1, one launch (start us, length us, event | category | flops | bytes accessed | tf_op | source)
XLA Modules:
  0.0 90.9 jit_solution(8782889931593325592)
XLA Ops:
  0.6 89.1 %shard_map.65.block_ref = f32[8,128]{1,0:T(8,128)} custom-call(bf16[32,1536]{1,0:T(8,128)(2,1)} %src_ref.1, bf16[16,1536]{1,0:T(8,128)(2,1)} %tgt_ref.1), custom_call_target="tpu_custom_call" | custom-call | flops 3053453312 | bytes 147456 | tf_op jit(solution)/shard_map/pallas_call | solution.py:657
  89.7 1.2 %shard_map.66 = (f32[1,32]{1,0:T(1,128)}, f32[1,16]{1,0:T(1,128)}, f32[1,32]{1,0:T(1,128)}, f32[1,16]{1,0:T(1,128)}, f32[1,1]{1,0:T(1,128)}) custom-call(f32[8,128]{1,0:T(8,128)} %shard_map.65.block_ref), custom_call_target="tpu_custom_call" | custom-call | tf_op jit(solution)/shard_map/pallas_call | solution.py:707

commit v4 on v3

--- a/solution.py
+++ b/solution.py
@@ -429,23 +429,31 @@
     def lanes_at(h, first=0):
         return slice(first + 128 * h, first + 128 * h + 128)
 
-    col_pot[0] = jnp.ones((8, 128), jnp.float32)
-    col_pot[1] = jnp.where(sub8 < 4, 0.0, 1.0)
-
     def iteration(index):
         def src_rows_part(r):
             at = pl.ds(r, 32)
-            values = [scores[at, lanes_at(h, cols_src)] + col_pot[1, h : h + 1] for h in range(lanes_tgt)]
-            top = tree(jnp.maximum, values)
-            best[at, :] = top
-            acc_cross[at, :] = tree(add, [jnp.exp2(v - top) for v in values])
+            values = [scores[at, lanes_at(h, cols_src)] for h in range(lanes_tgt)]
+            if index == 0:
+                top = tree(jnp.maximum, values)
+                best[at, :] = top
+                acc_cross[at, :] = tree(add, [jnp.exp2(v - top) for v in values])
+                acc[at, :] = tree(add, [scores[at, lanes_at(h)] for h in range(lanes_src)])
+                return
+            w = pot[at, :]
+            values = [jnp.exp2(v + w + col_pot[1, h : h + 1]) for h, v in enumerate(values)]
+            for h, v in enumerate(values):
+                scores[at, lanes_at(h, cols_src)] = v
+            acc_cross[at, :] = tree(add, values)
             acc[at, :] = tree(add, [scores[at, lanes_at(h)] * col_pot[0, h : h + 1] for h in range(lanes_src)])
 
         def tgt_rows_part(r):
             at = pl.ds(rows_src + r, 32)
             acc[at, :] = tree(
                 add,
-                [scores[at, lanes_at(h, cols_src)] * col_pot[1, 4 + h : 5 + h] for h in range(lanes_tgt)],
+                [
+                    scores[at, lanes_at(h, cols_src)] * (col_pot[1, 4 + h : 5 + h] if index else 1.0)
+                    for h in range(lanes_tgt)
+                ],
             )
 
         def in_parts(part):
@@ -463,7 +471,9 @@
 
         for r in range(blocks_src + blocks_tgt):
             at = slice(128 * r, 128 * r + 128)
-            if r < blocks_src:
+            if r < blocks_src and index:
+                row_send[index, r : r + 1] = over_sublanes(acc_cross[at, :].T, add, jnp.sum)
+            elif r < blocks_src:
                 each_top = best[at, :].T
                 top = over_sublanes(each_top, jnp.maximum, jnp.max)
                 total = over_sublanes(acc_cross[at, :].T * jnp.exp2(each_top - top), add, jnp.sum)
@@ -483,11 +493,16 @@
         others = row_recv.at[index, pl.ds(0, PLANE - 1), pl.ds(0, used_rows)]
         arrived(row_rs.at[index], others)
         parts = [row_recv[index, q] for q in range(PLANE)]
-        top = tree(jnp.maximum, parts)
-        spread = top + jnp.log2(tree(add, [jnp.exp2(p - top) for p in parts]))
-        phi = row_log - jnp.where(is_cross, spread, jnp.log2(tree(add, parts)))
+        change = row_log - jnp.log2(tree(add, parts))
+        if index == 0:
+            top = tree(jnp.maximum, parts)
+            spread = top + jnp.log2(tree(add, [jnp.exp2(p - top) for p in parts]))
+            phi = jnp.where(is_cross, row_log - spread, change)
+            table = jnp.where(is_cross, phi, jnp.exp2(phi))
+        else:
+            phi = jnp.where(is_cross, phi_ref[...] + change, change)
+            table = jnp.exp2(change)
         phi_ref[...] = phi
-        table = jnp.where(is_cross, phi, jnp.exp2(phi))
         table = jnp.concatenate([table, jnp.zeros((112, 128), jnp.float32)], axis=0).T
         for r in range(used_rows):
             pot[128 * r : 128 * r + 128, :] = jnp.broadcast_to(table[:, r : r + 1], (128, 128))
@@ -514,11 +529,14 @@
                 out += [new_top, total * jnp.exp2(top - new_top) + tree(add, parts)]
             return tuple(out)
 
-        start = (jnp.full((8, 128), -1e30, jnp.float32), jnp.zeros((8, 128), jnp.float32))
-        sums = over_rows(rows_src, cross_body, start * lanes_tgt)
-        tops = [jnp.max(t, axis=0, keepdims=True) for t in sums[::2]]
-        sums = [t * jnp.exp2(m - top) for t, m, top in zip(sums[1::2], sums[::2], tops)]
-        both = [tops[h] + jnp.log2(jnp.sum(sums[h], axis=0, keepdims=True)) for h in range(lanes_tgt)]
+        if index == 0:
+            start = (jnp.full((8, 128), -1e30, jnp.float32), jnp.zeros((8, 128), jnp.float32))
+            sums = over_rows(rows_src, cross_body, start * lanes_tgt)
+            tops = [jnp.max(t, axis=0, keepdims=True) for t in sums[::2]]
+            sums = [t * jnp.exp2(m - top) for t, m, top in zip(sums[1::2], sums[::2], tops)]
+            both = [tops[h] + jnp.log2(jnp.sum(sums[h], axis=0, keepdims=True)) for h in range(lanes_tgt)]
+        else:
+            both = weighted_cols(0, cols_src, 0, rows_src, lanes_tgt)
         both = both + weighted_cols(rows_src, cols_src, 2 * rows_src, rows_tgt, lanes_tgt)
         earlier = weighted_cols(0, 0, rows_src, rows_src, lanes_src)
         blocks = turned(jnp.concatenate(earlier, axis=0), jnp.concatenate(both, axis=0), chips_on)
@@ -555,7 +573,7 @@
         others = near_recv.at[index, pl.ds(0, 2 * NEAR - 1), pl.ds(0, size)]
         arrived(near_rs.at[index], others)
         me_far = 2 * z_far + core
-        block = merged([near_recv[index, q, 0:8] for q in range(2 * NEAR)], core == 1)
+        block = merged([near_recv[index, q, 0:8] for q in range(2 * NEAR)], None if index else core == 1)
         extra = tree(add, [near_recv[index, q, 8:9] for q in range(2 * NEAR)])
         far_send[index, 0:8] = block
         far_send[index, 8:9] = extra
@@ -577,25 +595,25 @@
         others = far_recv.at[index, pl.ds(0, 2 * FAR - 1), pl.ds(0, size)]
         arrived(far_rs.at[index], others)
         earlier = merged([far_recv[index, 2 * q, 0:8] for q in range(FAR)], None)
-        both = merged([far_recv[index, 2 * q + 1, 0:8] for q in range(FAR)], True)
+        both = merged([far_recv[index, 2 * q + 1, 0:8] for q in range(FAR)], None if index else True)
         totals[0] = earlier
         totals[1] = both
         totals[2, 0:1] = tree(add, [far_recv[index, 2 * q, 8:9] for q in range(FAR)])
 
-        @pl.when(index == 0)
-        def _():
+        if index == 0:
+            gamma = log_src - both
+            totals[3] = gamma
             earlier_pot, both_pot = turned(
-                n_src / earlier,
-                jnp.where(sub8 < 4, log_src - both, n_tgt / both),
-                lax.rem(NZ - chips_on, NZ),
+                n_src / earlier, jnp.where(sub8 < 4, gamma, n_tgt / both), lax.rem(NZ - chips_on, NZ)
             )
             col_pot[0] = earlier_pot
             col_pot[1] = both_pot
 
-    each(0, ITERS, iteration)
+    for index in range(ITERS):
+        iteration(index)
 
     earlier, both = totals[0], totals[1]
-    both = (1.0 / SCALE) * jnp.where(sub8 < 4, log_src - both, log_tgt - jnp.log2(both))
+    both = (1.0 / SCALE) * (jnp.where(sub8 < 4, totals[3] + log_src, log_tgt) - jnp.log2(both))
     earlier = (1.0 / SCALE) * (log_src - jnp.log2(earlier))
     share = jnp.where(sub8 < 4, 1.0 / n_tgt, -0.5 / n_tgt) * both - (0.5 / n_src) * earlier
     share = jnp.sum(share, axis=0, keepdims=True)
@@ -669,7 +687,7 @@
             pltpu.VMEM((2 * rows_src + rows_tgt, 128), f32),
             pltpu.VMEM((2, 8, 128), f32),
             pltpu.VMEM((16, 128), f32),
-            pltpu.VMEM((3, 8, 128), f32),
+            pltpu.VMEM((4, 8, 128), f32),
             pltpu.VMEM((ITERS, 16, 128), f32),
             pltpu.VMEM((ITERS, PLANE, 16, 128), f32),
             pltpu.VMEM((ITERS, 2, 16, 128), f32),

time: 91.1 us -> 90.5 us (level)
  no operation moved by 1% of the time
where the time goes in v4:
time: 90.5 us; the launch traced here: 90.3 us
  Pallas kernels  89.7 us (99%)
    pallas_call x1, Pallas kernels, per_device(): pl.pallas_call(kernel, out_shape=jax.ShapeDtypeStruct((8, 128), f32), in_...  88.5 us

profile of v4, /device:TPU:1, one launch (start us, length us, event | category | flops | bytes accessed | tf_op | source)
XLA Modules:
  0.0 90.3 jit_solution(10299200525250725700)
XLA Ops:
  0.6 88.5 %shard_map.65.block_ref = f32[8,128]{1,0:T(8,128)} custom-call(bf16[32,1536]{1,0:T(8,128)(2,1)} %src_ref.1, bf16[16,1536]{1,0:T(8,128)(2,1)} %tgt_ref.1), custom_call_target="tpu_custom_call" | custom-call | flops 3053453312 | bytes 147456 | tf_op jit(solution)/shard_map/pallas_call | solution.py:675
  89.1 1.2 %shard_map.66 = (f32[1,32]{1,0:T(1,128)}, f32[1,16]{1,0:T(1,128)}, f32[1,32]{1,0:T(1,128)}, f32[1,16]{1,0:T(1,128)}, f32[1,1]{1,0:T(1,128)}) custom-call(f32[8,128]{1,0:T(8,128)} %shard_map.65.block_ref), custom_call_target="tpu_custom_call" | custom-call | tf_op jit(solution)/shard_map/pallas_call | solution.py:725
